TPU v7x, 512 devices: a whole 4x4x16 slice. The times are simulated.
512 devices in a mesh: dom: 64 (over x, z), orb: 8 (over y, core).
Axes of the slice: x: 4, y: 4, z: 16, core: 2. Of those that a mesh axis runs over, the one named last changes fastest.
Arguments:
- orbitals: bfloat16 [3072, 64, 512], P('dom', 'orb'), may hold values from -6 to 6
- adjoint_source: bfloat16 [3072, 64, 512], P('dom', 'orb'), may hold values from -6 to 6
- eigenvalues: float32 [64], P('orb'), may hold values from -1 to -0.25
- cell_scale: float32 [3072], P('dom'), may hold values from 0.4 to 1.6
- base_potential: float32 [3072, 512], P('dom'), may hold values from 0.5 to 1.5
- stiffness: bfloat16 [512, 512], replicated, may hold values from -1.5 to 1.5, as said below
- face_perm: int32 [3072, 64], P('dom'), may hold values from 0 to 63, each once within a row
- restrict: bfloat16 [512, 64], replicated, may hold values from -0.25 to 0.25
- prolong: bfloat16 [64, 512], replicated, may hold values from -0.75 to 0.75
- owner: int32 [3072, 1], P('dom'), may hold values from 0 to 63; in each aligned block of 48 rows (0 to 47, 48 to 95, ...) at most 2 rows name the same one
- pot_slot: int32 [3072], P('dom'), may hold values from 0 to 63
- potential: float32 [4096, 64], P('dom'), may hold values from -6 to 6
Outputs:
- adjoint: bfloat16 [3072, 64, 512], P('dom', 'orb')
- updated: float32 [4096, 64], P('dom')
- applied: bfloat16 [3072, 64, 512], P('dom', 'orb')
Inputs may be any that keep to these rules, and one draw needn't show every extreme that they name: In the rows of one device no owner is named by more than 2 cells. `face_perm`: each row is a permutation. `stiffness`: symmetric.
All inputs are finite; a program needn't handle non-finite values.
Results may differ from a plain program's by a relative error of at most 0.0027.
Values sent between devices are 32-bit elements; how exact they have to be, the bound alone decides.
No kernel may reach another device: no remote copies, remote signals or barrier semaphores. Data moves between devices by JAX's collectives and lax.ppermute only.
A program may use at most 64 MiB of HBM per device.

v0:
```python
import jax
import jax.numpy as jnp
from jax import lax
from jax.sharding import PartitionSpec as P

ITERS = 4
relax = 0.25
step_rate = 0.1


def padded_2(block, sides, width):
    for axis, dim in sides:
        count = lax.axis_size(axis)
        forward = [(i, i + 1) for i in range(count - 1)]
        backward = [(target, source) for source, target in forward]
        low = lax.ppermute(
            lax.slice_in_dim(block, block.shape[dim] - width, None, axis=dim), axis, forward
        )
        high = lax.ppermute(lax.slice_in_dim(block, 0, width, axis=dim), axis, backward)
        block = jnp.concatenate([low, block, high], axis=dim)
    return block


def local(
    orbitals,
    adjoint_source,
    eigenvalues,
    cell_scale,
    base_potential,
    stiffness,
    face_perm,
    restrict,
    prolong,
    owner,
    pot_slot,
    potential,
):
    nodes = stiffness.shape[0]
    faces = face_perm.shape[1]
    pot_rows = potential.shape[0]
    n_domains = lax.axis_size("dom")
    cell_count = owner.shape[0]
    capacity = 2 * ((cell_count + n_domains - 1) // n_domains)
    onehot = (face_perm[:, :, None] == jnp.arange(faces, dtype=jnp.int32)[None, None, :]).astype(
        jnp.float32
    )

    def assemble_local(partial_sum):
        left_face = partial_sum[:, :, :faces]
        right_face = partial_sum[:, :, nodes - faces :]
        sent_right = jnp.einsum("ckj,cok->coj", onehot, right_face, precision=lax.Precision.HIGHEST)
        boundary = jnp.stack([left_face[0], sent_right[-1]], 0)
        padded = padded_2(boundary, (("dom", 0),), 1)
        left_next = jnp.concatenate([left_face[1:], padded[3][None]], 0)
        add_right = jnp.einsum("ckj,coj->cok", onehot, left_next, precision=lax.Precision.HIGHEST)
        add_left = jnp.concatenate([padded[0][None], sent_right[:-1]], 0)
        return jnp.concatenate(
            [
                left_face + add_left,
                partial_sum[:, :, faces : nodes - faces],
                right_face + add_right,
            ],
            2,
        )

    def operator(values_bf, values_full, shift):
        kinetic = jnp.dot(
            values_bf.reshape(-1, nodes), stiffness, preferred_element_type=jnp.float32
        ).reshape(values_full.shape)
        return assemble_local(cell_scale[:, None, None] * kinetic + shift * values_full)

    source = adjoint_source.astype(jnp.float32)
    shift = base_potential[:, None, :] - eigenvalues[None, :, None]
    iterate = relax * source
    for step_index in range(ITERS):
        image = operator(iterate.astype(jnp.bfloat16), iterate, shift)
        iterate = iterate + relax * (source - image)
    adjoint = iterate.astype(jnp.bfloat16)
    partial_density = jnp.sum(orbitals.astype(jnp.float32) * iterate, axis=1)
    restrict_full = restrict.astype(jnp.float32)
    density_term = lax.psum(partial_density, "orb")
    projected = jnp.dot(density_term, restrict_full, precision=lax.Precision.HIGHEST)
    coarse_cols = projected.shape[1]
    dest_owner = owner[:, 0]
    owner_hot = (dest_owner[:, None] == jnp.arange(n_domains, dtype=jnp.int32)[None, :]).astype(
        jnp.int32
    )
    earlier = jnp.cumsum(owner_hot, axis=0) - owner_hot
    rank_within = jnp.sum(earlier * owner_hot, axis=1)
    slot_index = dest_owner * capacity + rank_within
    send_hot_int = (
        slot_index[None, :] == jnp.arange(n_domains * capacity, dtype=jnp.int32)[:, None]
    ).astype(jnp.int32)
    send_hot = send_hot_int.astype(jnp.float32)
    send_values = jnp.dot(send_hot, projected, precision=lax.Precision.HIGHEST).reshape(
        n_domains, capacity, coarse_cols
    )
    send_ids = (jnp.sum(send_hot_int * (pot_slot + 1)[None, :], axis=1) - 1).reshape(
        n_domains, capacity
    )
    recv_values, recv_ids = (
        lax.all_to_all(send_values, "dom", split_axis=0, concat_axis=0, tiled=True),
        lax.all_to_all(send_ids, "dom", split_axis=0, concat_axis=0, tiled=True),
    )
    recv_hot = (
        recv_ids.reshape(-1)[None, :] == jnp.arange(pot_rows, dtype=jnp.int32)[:, None]
    ).astype(jnp.float32)
    summed = jnp.dot(
        recv_hot, recv_values.reshape(-1, coarse_cols), precision=lax.Precision.HIGHEST
    )
    updated = potential - step_rate * summed
    every_pot = lax.all_gather(updated, "dom", axis=0, tiled=True)
    cell_pot = every_pot[dest_owner * pot_rows + pot_slot]
    node_potential = jnp.dot(cell_pot, prolong.astype(jnp.float32), precision=lax.Precision.HIGHEST)
    shift_new = (base_potential + node_potential)[:, None, :]
    applied = operator(orbitals, orbitals.astype(jnp.float32), shift_new).astype(jnp.bfloat16)
    return (adjoint, updated, applied)


def solution(mesh):
    in_specs = (
        P("dom", "orb", None),
        P("dom", "orb", None),
        P("orb"),
        P("dom"),
        P("dom", None),
        P(),
        P("dom", None),
        P(),
        P(),
        P("dom", None),
        P("dom"),
        P("dom", None),
    )
    out_specs = (P("dom", "orb", None), P("dom", None), P("dom", "orb", None))
    return jax.shard_map(local, mesh=mesh, in_specs=in_specs, out_specs=out_specs, check_vma=False)
```

profile of v0, /device:TPU:2, one launch (start us, length us, event | category | flops | bytes accessed | tf_op | source)
XLA Modules:
  0.0 320.8 jit_solution(6365384118985894531)
XLA Ops:
  8.2 1.6 fusion.10
  9.8 11.4 %collective-permute-start.1 = (f32[1,8,64]{2,1,0:T(8,128)S(1)}, f32[1,8,64]{2,1,0:T(8,128)S(1)}, u32[]{:S(2)}, u32[]{:S(2)}) collective-permute-start(f32[1,8,64]{2,1,0:T(8,128)S(1)} %slice.159), channel_id=1, source_target_pairs={{8,0},{16,8},{24,16},{32,24},{40,32},{48,40},{56,48},{64,56},{72,6... | collective-permute-start | bytes 6152 | tf_op jit(solution)/shard_map/ppermute | solution.py:19
  22.7 1.9 collective-permute-start
  26.8 3.5 %collective-permute-done = f32[1,8,64]{2,1,0:T(8,128)S(1)} collective-permute-done((f32[1,8,64]{2,1,0:T(8,128)S(1)}, f32[1,8,64]{2,1,0:T(8,128)S(1)}, u32[]{:S(2)}, u32[]{:S(2)}) %collective-permute-start) | collective-permute-done | bytes 2080 | tf_op jit(solution)/shard_map/ppermute | solution.py:16
  31.2 2.6 collective-permute-start.3
  35.5 3.3 %collective-permute-start.2 = (f32[1,8,64]{2,1,0:T(8,128)S(1)}, f32[1,8,64]{2,1,0:T(8,128)S(1)}, u32[]{:S(2)}, u32[]{:S(2)}) collective-permute-start(f32[1,8,64]{2,1,0:T(8,128)S(1)} %slice.162), channel_id=1, source_target_pairs={{0,8},{8,16},{16,24},{24,32},{32,40},{40,48},{48,56},{56,64},{64,7... | collective-permute-start | bytes 6152 | tf_op jit(solution)/shard_map/ppermute | solution.py:16
  40.2 2.9 collective-permute-done.2
  44.2 1.9 collective-permute-start.5
  47.8 3.9 %collective-permute-start.4 = (f32[1,8,64]{2,1,0:T(8,128)S(1)}, f32[1,8,64]{2,1,0:T(8,128)S(1)}, u32[]{:S(2)}, u32[]{:S(2)}) collective-permute-start(f32[1,8,64]{2,1,0:T(8,128)S(1)} %slice.169), channel_id=1, source_target_pairs={{0,8},{8,16},{16,24},{24,32},{32,40},{40,48},{48,56},{56,64},{64,7... | collective-permute-start | bytes 6152 | tf_op jit(solution)/shard_map/ppermute | solution.py:16
  53.2 2.3 collective-permute-done.4
  56.3 1.9 collective-permute-start.7
  60.0 3.9 %collective-permute-start.6 = (f32[1,8,64]{2,1,0:T(8,128)S(1)}, f32[1,8,64]{2,1,0:T(8,128)S(1)}, u32[]{:S(2)}, u32[]{:S(2)}) collective-permute-start(f32[1,8,64]{2,1,0:T(8,128)S(1)} %slice.176), channel_id=1, source_target_pairs={{0,8},{8,16},{16,24},{24,32},{32,40},{40,48},{48,56},{56,64},{64,7... | collective-permute-start | bytes 6152 | tf_op jit(solution)/shard_map/ppermute | solution.py:16
  65.3 2.3 collective-permute-done.6
  67.7 2.1 fusion.24
  70.5 5.7 %all-to-all-start = ((s32[64,1,2]{2,1,0:T(1,128)}), s32[64,1,2]{2,1,0:T(1,128)S(1)}, u32[]{:S(2)}, u32[]{:S(2)}) async-start(s32[64,1,2]{2,1,0:T(1,128)} %bitcast.2), calls=%async_computation | async-start | bytes 65536 | tf_op jit(solution)/shard_map/all_to_all | solution.py:103
  76.3 58.1 %all-reduce.2.cloned.1.call-done = f32[48,512]{1,0:T(8,128)} async-done(((f32[48,512]{1,0:T(8,128)}), f32[48,512]{1,0:T(8,128)}) %all-reduce.2.cloned.1.call-update) | async-done | bytes 98320 | tf_op jit(solution)/shard_map/psum | solution.py:81
  136.5 15.9 %all-to-all-start.1 = ((f32[64,1,128]{2,1,0:T(1,128)}), f32[64,1,128]{2,1,0:T(1,128)S(1)}, u32[]{:S(2)}, u32[]{:S(2)}) async-start(f32[64,1,128]{2,1,0:T(1,128)} %reshape.85), calls=%async_computation.1 | async-start | bytes 65536 | tf_op jit(solution)/shard_map/all_to_all | solution.py:102
  153.8 12.0 %all-to-all-done.1 = f32[64,1,128]{2,1,0:T(1,128)S(1)} async-done(((f32[64,1,128]{2,1,0:T(1,128)}), f32[64,1,128]{2,1,0:T(1,128)S(1)}, u32[]{:S(2)}, u32[]{:S(2)}) %all-to-all-start.1) | async-done | bytes 32800 | tf_op jit(solution)/shard_map/all_to_all | solution.py:102
  168.0 128.1 %all-gather.2.cloned.1.call-done = f32[4096,64]{1,0:T(8,128)} async-done(((f32[64,64]{1,0:T(8,128)}), f32[4096,64]{1,0:T(8,128)}) %all-gather.2.cloned.1.call-update) | async-done | bytes 1048592 | tf_op jit(solution)/shard_map/all_gather | solution.py:112
  296.1 2.2 gather_fusion
  298.9 4.8 %collective-permute-start.9 = (f32[1,8,64]{2,1,0:T(8,128)S(1)}, f32[1,8,64]{2,1,0:T(8,128)S(1)}, u32[]{:S(2)}, u32[]{:S(2)}) collective-permute-start(f32[1,8,64]{2,1,0:T(8,128)S(1)} %slice.187), channel_id=1, source_target_pairs={{8,0},{16,8},{24,16},{32,24},{40,32},{48,40},{56,48},{64,56},{72,6... | collective-permute-start | bytes 6152 | tf_op jit(solution)/shard_map/ppermute | solution.py:19
  305.4 1.9 collective-permute-start.8
  307.3 1.6 fusion.20
  308.9 4.1 %collective-permute-done.8 = f32[1,8,64]{2,1,0:T(8,128)S(1)} collective-permute-done((f32[1,8,64]{2,1,0:T(8,128)S(1)}, f32[1,8,64]{2,1,0:T(8,128)S(1)}, u32[]{:S(2)}, u32[]{:S(2)}) %collective-permute-start.8) | collective-permute-done | bytes 2080 | tf_op jit(solution)/shard_map/ppermute | solution.py:16
  (98 shorter events, 26.3 us)
Async XLA Ops:
  7.2 14.0 %copy-start.11 = (s32[48,64]{1,0:T(8,128)S(1)}, s32[48,64]{1,0:T(8,128)}, u32[]{:S(2)}) copy-start(s32[48,64]{1,0:T(8,128)} %param.18) | copy-start | bytes 36868
  7.2 17.4 %copy-start.7 = (s32[48,1]{0,1:T(1,128)S(1)}, s32[48,1]{0,1:T(1,128)}, u32[]{:S(2)}) copy-start(s32[48,1]{0,1:T(1,128)} %param.21) | copy-start | bytes 580
  7.2 17.7 %copy-start.9 = (s32[48]{0:T(128)S(1)}, s32[48]{0:T(128)}, u32[]{:S(2)}) copy-start(s32[48]{0:T(128)} %param.22) | copy-start | bytes 580
  7.2 127.1 %all-reduce.2.cloned.1.call-start = ((), (), s32[]{:S(2)}) async-start(), calls=%async_computation.2 | async-start | bytes 196608 | tf_op jit(solution)/shard_map/psum | solution.py:81
  9.8 15.5 %collective-permute-start.1 = (f32[1,8,64]{2,1,0:T(8,128)S(1)}, f32[1,8,64]{2,1,0:T(8,128)S(1)}, u32[]{:S(2)}, u32[]{:S(2)}) collective-permute-start(f32[1,8,64]{2,1,0:T(8,128)S(1)} %slice.159), channel_id=1, source_target_pairs={{8,0},{16,8},{24,16},{32,24},{40,32},{48,40},{56,48},{64,56},{72,6... | collective-permute-start | bytes 6152 | tf_op jit(solution)/shard_map/ppermute | solution.py:19
  22.7 7.6 %collective-permute-start = (f32[1,8,64]{2,1,0:T(8,128)S(1)}, f32[1,8,64]{2,1,0:T(8,128)S(1)}, u32[]{:S(2)}, u32[]{:S(2)}) collective-permute-start(f32[1,8,64]{2,1,0:T(8,128)S(1)} %slice.155), channel_id=1, source_target_pairs={{0,8},{8,16},{16,24},{24,32},{32,40},{40,48},{48,56},{56,64},{64,7... | collective-permute-start | bytes 6152 | tf_op jit(solution)/shard_map/ppermute | solution.py:16
  25.0 5.3 %copy-start.1 = (bf16[48,8,512]{2,1,0:T(8,128)(2,1)S(1)}, bf16[48,8,512]{2,1,0:T(8,128)(2,1)}, u32[]{:S(2)}) copy-start(bf16[48,8,512]{2,1,0:T(8,128)(2,1)} %param.13) | copy-start | bytes 1179652
  25.1 5.3 %copy-start.3 = (f32[48,512]{1,0:T(8,128)S(1)}, f32[48,512]{1,0:T(8,128)}, u32[]{:S(2)}) copy-start(f32[48,512]{1,0:T(8,128)} %param.16) | copy-start | bytes 294916
  25.1 5.3 %copy-start.8 = (f32[48]{0:T(128)S(1)}, f32[48]{0:T(128)}, u32[]{:S(2)}) copy-start(f32[48]{0:T(128)} %param.15) | copy-start | bytes 580
  31.2 7.6 %collective-permute-start.3 = (f32[1,8,64]{2,1,0:T(8,128)S(1)}, f32[1,8,64]{2,1,0:T(8,128)S(1)}, u32[]{:S(2)}, u32[]{:S(2)}) collective-permute-start(f32[1,8,64]{2,1,0:T(8,128)S(1)} %slice.166), channel_id=1, source_target_pairs={{8,0},{16,8},{24,16},{32,24},{40,32},{48,40},{56,48},{64,56},{72,6... | collective-permute-start | bytes 6152 | tf_op jit(solution)/shard_map/ppermute | solution.py:19
  35.5 7.6 %collective-permute-start.2 = (f32[1,8,64]{2,1,0:T(8,128)S(1)}, f32[1,8,64]{2,1,0:T(8,128)S(1)}, u32[]{:S(2)}, u32[]{:S(2)}) collective-permute-start(f32[1,8,64]{2,1,0:T(8,128)S(1)} %slice.162), channel_id=1, source_target_pairs={{0,8},{8,16},{16,24},{24,32},{32,40},{40,48},{48,56},{56,64},{64,7... | collective-permute-start | bytes 6152 | tf_op jit(solution)/shard_map/ppermute | solution.py:16
  44.2 7.6 %collective-permute-start.5 = (f32[1,8,64]{2,1,0:T(8,128)S(1)}, f32[1,8,64]{2,1,0:T(8,128)S(1)}, u32[]{:S(2)}, u32[]{:S(2)}) collective-permute-start(f32[1,8,64]{2,1,0:T(8,128)S(1)} %slice.173), channel_id=1, source_target_pairs={{8,0},{16,8},{24,16},{32,24},{40,32},{48,40},{56,48},{64,56},{72,6... | collective-permute-start | bytes 6152 | tf_op jit(solution)/shard_map/ppermute | solution.py:19
  47.8 7.6 %collective-permute-start.4 = (f32[1,8,64]{2,1,0:T(8,128)S(1)}, f32[1,8,64]{2,1,0:T(8,128)S(1)}, u32[]{:S(2)}, u32[]{:S(2)}) collective-permute-start(f32[1,8,64]{2,1,0:T(8,128)S(1)} %slice.169), channel_id=1, source_target_pairs={{0,8},{8,16},{16,24},{24,32},{32,40},{40,48},{48,56},{56,64},{64,7... | collective-permute-start | bytes 6152 | tf_op jit(solution)/shard_map/ppermute | solution.py:16
  56.3 7.6 %collective-permute-start.7 = (f32[1,8,64]{2,1,0:T(8,128)S(1)}, f32[1,8,64]{2,1,0:T(8,128)S(1)}, u32[]{:S(2)}, u32[]{:S(2)}) collective-permute-start(f32[1,8,64]{2,1,0:T(8,128)S(1)} %slice.180), channel_id=1, source_target_pairs={{8,0},{16,8},{24,16},{32,24},{40,32},{48,40},{56,48},{64,56},{72,6... | collective-permute-start | bytes 6152 | tf_op jit(solution)/shard_map/ppermute | solution.py:19
  59.7 8.0 %copy-start.2 = (bf16[48,8,512]{2,1,0:T(8,128)(2,1)S(1)}, bf16[48,8,512]{2,1,0:T(8,128)(2,1)}, u32[]{:S(2)}) copy-start(bf16[48,8,512]{2,1,0:T(8,128)(2,1)} %param.12) | copy-start | bytes 1179652
  60.0 7.6 %collective-permute-start.6 = (f32[1,8,64]{2,1,0:T(8,128)S(1)}, f32[1,8,64]{2,1,0:T(8,128)S(1)}, u32[]{:S(2)}, u32[]{:S(2)}) collective-permute-start(f32[1,8,64]{2,1,0:T(8,128)S(1)} %slice.176), channel_id=1, source_target_pairs={{0,8},{8,16},{16,24},{24,32},{32,40},{40,48},{48,56},{56,64},{64,7... | collective-permute-start | bytes 6152 | tf_op jit(solution)/shard_map/ppermute | solution.py:16
  67.6 66.7 %copy-start.4 = (bf16[512,64]{0,1:T(8,128)(2,1)S(1)}, bf16[512,64]{0,1:T(8,128)(2,1)}, u32[]{:S(2)}) copy-start(bf16[512,64]{0,1:T(8,128)(2,1)} %param.19) | copy-start | bytes 196612
  67.7 99.5 %copy-start.6 = (f32[64,64]{1,0:T(8,128)S(1)}, f32[64,64]{1,0:T(8,128)}, u32[]{:S(2)}) copy-start(f32[64,64]{1,0:T(8,128)} %param.23) | copy-start | bytes 49156
  67.7 230.6 %copy-start.5 = (bf16[64,512]{1,0:T(8,128)(2,1)S(1)}, bf16[64,512]{1,0:T(8,128)(2,1)}, u32[]{:S(2)}) copy-start(bf16[64,512]{1,0:T(8,128)(2,1)} %param.20) | copy-start | bytes 196612
  70.5 65.9 %all-to-all-start = ((s32[64,1,2]{2,1,0:T(1,128)}), s32[64,1,2]{2,1,0:T(1,128)S(1)}, u32[]{:S(2)}, u32[]{:S(2)}) async-start(s32[64,1,2]{2,1,0:T(1,128)} %bitcast.2), calls=%async_computation | async-start | bytes 65536 | tf_op jit(solution)/shard_map/all_to_all | solution.py:103
  136.5 29.4 %all-to-all-start.1 = ((f32[64,1,128]{2,1,0:T(1,128)}), f32[64,1,128]{2,1,0:T(1,128)S(1)}, u32[]{:S(2)}, u32[]{:S(2)}) async-start(f32[64,1,128]{2,1,0:T(1,128)} %reshape.85), calls=%async_computation.1 | async-start | bytes 65536 | tf_op jit(solution)/shard_map/all_to_all | solution.py:102
  152.4 143.7 %all-gather.2.cloned.1.call-start = ((), (), s32[]{:S(2)}) async-start(), calls=%async_computation.3 | async-start | bytes 2129920 | tf_op jit(solution)/shard_map/all_gather | solution.py:112
  298.9 8.4 %collective-permute-start.9 = (f32[1,8,64]{2,1,0:T(8,128)S(1)}, f32[1,8,64]{2,1,0:T(8,128)S(1)}, u32[]{:S(2)}, u32[]{:S(2)}) collective-permute-start(f32[1,8,64]{2,1,0:T(8,128)S(1)} %slice.187), channel_id=1, source_target_pairs={{8,0},{16,8},{24,16},{32,24},{40,32},{48,40},{56,48},{64,56},{72,6... | collective-permute-start | bytes 6152 | tf_op jit(solution)/shard_map/ppermute | solution.py:19
  305.4 7.6 %collective-permute-start.8 = (f32[1,8,64]{2,1,0:T(8,128)S(1)}, f32[1,8,64]{2,1,0:T(8,128)S(1)}, u32[]{:S(2)}, u32[]{:S(2)}) collective-permute-start(f32[1,8,64]{2,1,0:T(8,128)S(1)} %slice.183), channel_id=1, source_target_pairs={{0,8},{8,16},{16,24},{24,32},{32,40},{40,48},{48,56},{56,64},{64,7... | collective-permute-start | bytes 6152 | tf_op jit(solution)/shard_map/ppermute | solution.py:16
  (2 other events, 6.3 us)
Sparse Core Ops, SparseCore 0:
  69.9 64.3 all-reduce.1
  168.1 127.9 all-gather.1
where the time goes:
time: 321 us
  waiting for transfers between devices  213 us (66%)
  starting transfers between devices  59.2 us (18%)
  matrix products  20.7 us (6%)
  between operations  14.7 us (5%)
  local copies, waits for them, and re-layouts  7.21 us (2%)
  other arithmetic  5.72 us (2%)
    all_gather x1, waiting for transfers between devices, local(): every_pot = lax.all_gather(updated, 'dom', axis=0, tiled=True)  128 us
    psum x1, waiting for transfers between devices, local(): density_term = lax.psum(partial_density, 'orb')  58.1 us
    ppermute x5, starting transfers between devices, padded_2(): lax.ppermute(lax.slice_in_dim(block, 0, width, axis=dim), axis, backward)  22.6 us
    all_to_all x1, starting transfers between devices, local(): lax.all_to_all(send_values, 'dom', split_axis=0, concat_axis=0, tiled=True)  15.9 us
    ppermute x5, waiting for transfers between devices, padded_2(): lax.ppermute(lax.slice_in_dim(block, block.shape[dim] - width, None, axis...  15 us
    ppermute x5, starting transfers between devices, padded_2(): lax.ppermute(lax.slice_in_dim(block, block.shape[dim] - width, None, axis...  15 us
    all_to_all x1, waiting for transfers between devices, local(): lax.all_to_all(send_values, 'dom', split_axis=0, concat_axis=0, tiled=True)  12 us
    dot_general x5, matrix products, assemble_local(): jnp.einsum('ckj,coj->cok', onehot, left_next, precision=lax.Precision.HIG...  7.2 us
  transfers between devices with their start and end apart: 14, of which 8 were waited for; matrix products, arithmetic and copies ran while one was open for 6% of the time, Pallas kernels for 0%

commit v1 on v0

--- a/solution.py
+++ b/solution.py
@@ -78,7 +78,7 @@
     adjoint = iterate.astype(jnp.bfloat16)
     partial_density = jnp.sum(orbitals.astype(jnp.float32) * iterate, axis=1)
     restrict_full = restrict.astype(jnp.float32)
-    density_term = lax.psum(partial_density, "orb")
+    density_term = jnp.sum(lax.all_gather(partial_density, "orb"), axis=0)
     projected = jnp.dot(density_term, restrict_full, precision=lax.Precision.HIGHEST)
     coarse_cols = projected.shape[1]
     dest_owner = owner[:, 0]

time: 321 us -> 279 us (0.87)
  waiting for transfers between devices: 213 us -> 157 us
  blocking collectives: 0 us -> 14.3 us
    psum x1 -> x0, waiting for transfers between devices: 58.1 us -> none  [local(): density_term = lax.psum(partial_density, 'orb')]
    all_gather x0 -> x1, blocking collectives: none -> 14.3 us  [local(): density_term = jnp.sum(lax.all_gather(partial_density, 'orb'), axis=0)]
    all_to_all x1, starting transfers between devices: 5.7 us -> 18.6 us  [local(): lax.all_to_all(send_ids, 'dom', split_axis=0, concat_axis=0, tiled=True)]
    ppermute x5, starting transfers between devices: 22.6 us -> 15.3 us  [padded_2(): lax.ppermute(lax.slice_in_dim(block, 0, width, axis=dim), axis, backward)]
    all_to_all x1, starting transfers between devices: 15.9 us -> 9.42 us  [local(): lax.all_to_all(send_values, 'dom', split_axis=0, concat_axis=0, tiled=True)]
  transfers between devices with their start and end apart: 14 -> 13, of which waited for: 8 -> 7; matrix products, arithmetic and copies ran while one was open for 6% -> 9% of each run, Pallas kernels for 0% -> 0%
where the time goes in v1:
time: 279 us; the launch traced here: 278 us
  waiting for transfers between devices  157 us (56%)
  starting transfers between devices  59 us (21%)
  matrix products  19.8 us (7%)
  between operations  14.6 us (5%)
  blocking collectives  14.3 us (5%)
  other arithmetic  7.18 us (3%)
  local copies, waits for them, and re-layouts  6.25 us (2%)
    all_gather x1, waiting for transfers between devices, local(): every_pot = lax.all_gather(updated, 'dom', axis=0, tiled=True)  130 us
    all_to_all x1, starting transfers between devices, local(): lax.all_to_all(send_ids, 'dom', split_axis=0, concat_axis=0, tiled=True)  18.6 us
    ppermute x5, starting transfers between devices, padded_2(): lax.ppermute(lax.slice_in_dim(block, block.shape[dim] - width, None, axis...  15.6 us
    ppermute x5, starting transfers between devices, padded_2(): lax.ppermute(lax.slice_in_dim(block, 0, width, axis=dim), axis, backward)  15.3 us
    ppermute x5, waiting for transfers between devices, padded_2(): lax.ppermute(lax.slice_in_dim(block, block.shape[dim] - width, None, axis...  15 us
    all_gather x1, blocking collectives, local(): density_term = jnp.sum(lax.all_gather(partial_density, 'orb'), axis=0)  14.3 us
    all_to_all x1, waiting for transfers between devices, local(): lax.all_to_all(send_values, 'dom', split_axis=0, concat_axis=0, tiled=True)  12 us
    all_to_all x1, starting transfers between devices, local(): lax.all_to_all(send_values, 'dom', split_axis=0, concat_axis=0, tiled=True)  9.42 us
  transfers between devices with their start and end apart: 13, of which 7 were waited for; matrix products, arithmetic and copies ran while one was open for 9% of the time, Pallas kernels for 0%

profile of v1, /device:TPU:2, one launch (start us, length us, event | category | flops | bytes accessed | tf_op | source)
XLA Modules:
  0.0 278.3 jit_solution(2145143908049543588)
XLA Ops:
  10.4 18.6 %all-to-all-start = ((s32[64,1,2]{2,1,0:T(1,128)}), s32[64,1,2]{2,1,0:T(1,128)S(1)}, u32[]{:S(2)}, u32[]{:S(2)}) async-start(s32[64,1,2]{2,1,0:T(1,128)} %bitcast.2), calls=%async_computation | async-start | bytes 65536 | tf_op jit(solution)/shard_map/all_to_all | solution.py:103
  29.1 1.6 fusion.10
  30.7 4.6 %collective-permute-start.1 = (f32[1,8,64]{2,1,0:T(8,128)S(1)}, f32[1,8,64]{2,1,0:T(8,128)S(1)}, u32[]{:S(2)}, u32[]{:S(2)}) collective-permute-start(f32[1,8,64]{2,1,0:T(8,128)S(1)} %slice.159), channel_id=1, source_target_pairs={{8,0},{16,8},{24,16},{32,24},{40,32},{48,40},{56,48},{64,56},{72,6... | collective-permute-start | bytes 6152 | tf_op jit(solution)/shard_map/ppermute | solution.py:19
  36.8 2.1 collective-permute-start
  40.5 4.0 %collective-permute-done = f32[1,8,64]{2,1,0:T(8,128)S(1)} collective-permute-done((f32[1,8,64]{2,1,0:T(8,128)S(1)}, f32[1,8,64]{2,1,0:T(8,128)S(1)}, u32[]{:S(2)}, u32[]{:S(2)}) %collective-permute-start) | collective-permute-done | bytes 2080 | tf_op jit(solution)/shard_map/ppermute | solution.py:16
  45.5 2.1 collective-permute-start.3
  49.3 3.8 %collective-permute-start.2 = (f32[1,8,64]{2,1,0:T(8,128)S(1)}, f32[1,8,64]{2,1,0:T(8,128)S(1)}, u32[]{:S(2)}, u32[]{:S(2)}) collective-permute-start(f32[1,8,64]{2,1,0:T(8,128)S(1)} %slice.162), channel_id=1, source_target_pairs={{0,8},{8,16},{16,24},{24,32},{32,40},{40,48},{48,56},{56,64},{64,7... | collective-permute-start | bytes 6152 | tf_op jit(solution)/shard_map/ppermute | solution.py:16
  54.5 2.4 collective-permute-done.2
  57.9 1.9 collective-permute-start.5
  61.6 3.9 %collective-permute-start.4 = (f32[1,8,64]{2,1,0:T(8,128)S(1)}, f32[1,8,64]{2,1,0:T(8,128)S(1)}, u32[]{:S(2)}, u32[]{:S(2)}) collective-permute-start(f32[1,8,64]{2,1,0:T(8,128)S(1)} %slice.169), channel_id=1, source_target_pairs={{0,8},{8,16},{16,24},{24,32},{32,40},{40,48},{48,56},{56,64},{64,7... | collective-permute-start | bytes 6152 | tf_op jit(solution)/shard_map/ppermute | solution.py:16
  66.9 2.3 collective-permute-done.4
  70.1 1.9 collective-permute-start.7
  73.7 3.9 %collective-permute-start.6 = (f32[1,8,64]{2,1,0:T(8,128)S(1)}, f32[1,8,64]{2,1,0:T(8,128)S(1)}, u32[]{:S(2)}, u32[]{:S(2)}) collective-permute-start(f32[1,8,64]{2,1,0:T(8,128)S(1)} %slice.176), channel_id=1, source_target_pairs={{0,8},{8,16},{16,24},{24,32},{32,40},{40,48},{48,56},{56,64},{64,7... | collective-permute-start | bytes 6152 | tf_op jit(solution)/shard_map/ppermute | solution.py:16
  79.1 2.3 collective-permute-done.6
  81.4 1.4 fusion.24
  82.8 14.3 %all-gather = f32[384,512]{1,0:T(8,128)S(1)} all-gather(f32[48,512]{1,0:T(8,128)S(1)} %get-tuple-element.3), channel_id=2, replica_groups=mesh['dom'=64,'orb'=8] {'orb'}, dimensions={0}, use_global_device_ids=true | all-gather | bytes 884736 | tf_op jit(solution)/shard_map/all_gather | solution.py:81
  98.5 9.4 %all-to-all-start.1 = ((f32[64,1,128]{2,1,0:T(1,128)}), f32[64,1,128]{2,1,0:T(1,128)S(1)}, u32[]{:S(2)}, u32[]{:S(2)}) async-start(f32[64,1,128]{2,1,0:T(1,128)} %reshape.86), calls=%async_computation.1 | async-start | bytes 65536 | tf_op jit(solution)/shard_map/all_to_all | solution.py:102
  109.3 12.0 %all-to-all-done.1 = f32[64,1,128]{2,1,0:T(1,128)S(1)} async-done(((f32[64,1,128]{2,1,0:T(1,128)}), f32[64,1,128]{2,1,0:T(1,128)S(1)}, u32[]{:S(2)}, u32[]{:S(2)}) %all-to-all-start.1) | async-done | bytes 32800 | tf_op jit(solution)/shard_map/all_to_all | solution.py:102
  123.5 130.0 %all-gather.3.cloned.1.call-done = f32[4096,64]{1,0:T(8,128)} async-done(((f32[64,64]{1,0:T(8,128)}), f32[4096,64]{1,0:T(8,128)}) %all-gather.3.cloned.1.call-update) | async-done | bytes 1048592 | tf_op jit(solution)/shard_map/all_gather | solution.py:112
  253.5 2.2 gather_fusion
  256.3 4.8 %collective-permute-start.9 = (f32[1,8,64]{2,1,0:T(8,128)S(1)}, f32[1,8,64]{2,1,0:T(8,128)S(1)}, u32[]{:S(2)}, u32[]{:S(2)}) collective-permute-start(f32[1,8,64]{2,1,0:T(8,128)S(1)} %slice.187), channel_id=1, source_target_pairs={{8,0},{16,8},{24,16},{32,24},{40,32},{48,40},{56,48},{64,56},{72,6... | collective-permute-start | bytes 6152 | tf_op jit(solution)/shard_map/ppermute | solution.py:19
  262.8 1.9 collective-permute-start.8
  264.7 1.6 fusion.20
  266.3 4.1 %collective-permute-done.8 = f32[1,8,64]{2,1,0:T(8,128)S(1)} collective-permute-done((f32[1,8,64]{2,1,0:T(8,128)S(1)}, f32[1,8,64]{2,1,0:T(8,128)S(1)}, u32[]{:S(2)}, u32[]{:S(2)}) %collective-permute-start.8) | collective-permute-done | bytes 2080 | tf_op jit(solution)/shard_map/ppermute | solution.py:16
  (93 shorter events, 26.5 us)
Async XLA Ops:
  7.2 21.9 %copy-start = (bf16[512,512]{1,0:T(8,128)(2,1)S(1)}, bf16[512,512]{1,0:T(8,128)(2,1)}, u32[]{:S(2)}) copy-start(bf16[512,512]{1,0:T(8,128)(2,1)} %param.17) | copy-start | bytes 1572868
  7.2 28.1 %copy-start.9 = (s32[48,64]{1,0:T(8,128)S(1)}, s32[48,64]{1,0:T(8,128)}, u32[]{:S(2)}) copy-start(s32[48,64]{1,0:T(8,128)} %param.18) | copy-start | bytes 36868
  10.4 88.0 %all-to-all-start = ((s32[64,1,2]{2,1,0:T(1,128)}), s32[64,1,2]{2,1,0:T(1,128)S(1)}, u32[]{:S(2)}, u32[]{:S(2)}) async-start(s32[64,1,2]{2,1,0:T(1,128)} %bitcast.2), calls=%async_computation | async-start | bytes 65536 | tf_op jit(solution)/shard_map/all_to_all | solution.py:103
  30.7 8.4 %collective-permute-start.1 = (f32[1,8,64]{2,1,0:T(8,128)S(1)}, f32[1,8,64]{2,1,0:T(8,128)S(1)}, u32[]{:S(2)}, u32[]{:S(2)}) collective-permute-start(f32[1,8,64]{2,1,0:T(8,128)S(1)} %slice.159), channel_id=1, source_target_pairs={{8,0},{16,8},{24,16},{32,24},{40,32},{48,40},{56,48},{64,56},{72,6... | collective-permute-start | bytes 6152 | tf_op jit(solution)/shard_map/ppermute | solution.py:19
  36.7 7.8 %copy-start.1 = (bf16[48,8,512]{2,1,0:T(8,128)(2,1)S(1)}, bf16[48,8,512]{2,1,0:T(8,128)(2,1)}, u32[]{:S(2)}) copy-start(bf16[48,8,512]{2,1,0:T(8,128)(2,1)} %param.13) | copy-start | bytes 1179652
  36.8 7.8 %copy-start.3 = (f32[48,512]{1,0:T(8,128)S(1)}, f32[48,512]{1,0:T(8,128)}, u32[]{:S(2)}) copy-start(f32[48,512]{1,0:T(8,128)} %param.16) | copy-start | bytes 294916
  36.8 7.8 %copy-start.7 = (f32[48]{0:T(128)S(1)}, f32[48]{0:T(128)}, u32[]{:S(2)}) copy-start(f32[48]{0:T(128)} %param.15) | copy-start | bytes 580
  36.8 7.8 %copy-start.8 = (f32[8]{0:T(128)S(1)}, f32[8]{0:T(128)}, u32[]{:S(2)}) copy-start(f32[8]{0:T(128)} %param.14) | copy-start | bytes 100
  36.8 7.7 %collective-permute-start = (f32[1,8,64]{2,1,0:T(8,128)S(1)}, f32[1,8,64]{2,1,0:T(8,128)S(1)}, u32[]{:S(2)}, u32[]{:S(2)}) collective-permute-start(f32[1,8,64]{2,1,0:T(8,128)S(1)} %slice.155), channel_id=1, source_target_pairs={{0,8},{8,16},{16,24},{24,32},{32,40},{40,48},{48,56},{56,64},{64,7... | collective-permute-start | bytes 6152 | tf_op jit(solution)/shard_map/ppermute | solution.py:16
  45.5 7.6 %collective-permute-start.3 = (f32[1,8,64]{2,1,0:T(8,128)S(1)}, f32[1,8,64]{2,1,0:T(8,128)S(1)}, u32[]{:S(2)}, u32[]{:S(2)}) collective-permute-start(f32[1,8,64]{2,1,0:T(8,128)S(1)} %slice.166), channel_id=1, source_target_pairs={{8,0},{16,8},{24,16},{32,24},{40,32},{48,40},{56,48},{64,56},{72,6... | collective-permute-start | bytes 6152 | tf_op jit(solution)/shard_map/ppermute | solution.py:19
  49.3 7.6 %collective-permute-start.2 = (f32[1,8,64]{2,1,0:T(8,128)S(1)}, f32[1,8,64]{2,1,0:T(8,128)S(1)}, u32[]{:S(2)}, u32[]{:S(2)}) collective-permute-start(f32[1,8,64]{2,1,0:T(8,128)S(1)} %slice.162), channel_id=1, source_target_pairs={{0,8},{8,16},{16,24},{24,32},{32,40},{40,48},{48,56},{56,64},{64,7... | collective-permute-start | bytes 6152 | tf_op jit(solution)/shard_map/ppermute | solution.py:16
  57.9 7.6 %collective-permute-start.5 = (f32[1,8,64]{2,1,0:T(8,128)S(1)}, f32[1,8,64]{2,1,0:T(8,128)S(1)}, u32[]{:S(2)}, u32[]{:S(2)}) collective-permute-start(f32[1,8,64]{2,1,0:T(8,128)S(1)} %slice.173), channel_id=1, source_target_pairs={{8,0},{16,8},{24,16},{32,24},{40,32},{48,40},{56,48},{64,56},{72,6... | collective-permute-start | bytes 6152 | tf_op jit(solution)/shard_map/ppermute | solution.py:19
  61.6 7.6 %collective-permute-start.4 = (f32[1,8,64]{2,1,0:T(8,128)S(1)}, f32[1,8,64]{2,1,0:T(8,128)S(1)}, u32[]{:S(2)}, u32[]{:S(2)}) collective-permute-start(f32[1,8,64]{2,1,0:T(8,128)S(1)} %slice.169), channel_id=1, source_target_pairs={{0,8},{8,16},{16,24},{24,32},{32,40},{40,48},{48,56},{56,64},{64,7... | collective-permute-start | bytes 6152 | tf_op jit(solution)/shard_map/ppermute | solution.py:16
  70.1 7.6 %collective-permute-start.7 = (f32[1,8,64]{2,1,0:T(8,128)S(1)}, f32[1,8,64]{2,1,0:T(8,128)S(1)}, u32[]{:S(2)}, u32[]{:S(2)}) collective-permute-start(f32[1,8,64]{2,1,0:T(8,128)S(1)} %slice.180), channel_id=1, source_target_pairs={{8,0},{16,8},{24,16},{32,24},{40,32},{48,40},{56,48},{64,56},{72,6... | collective-permute-start | bytes 6152 | tf_op jit(solution)/shard_map/ppermute | solution.py:19
  73.4 8.0 %copy-start.2 = (bf16[48,8,512]{2,1,0:T(8,128)(2,1)S(1)}, bf16[48,8,512]{2,1,0:T(8,128)(2,1)}, u32[]{:S(2)}) copy-start(bf16[48,8,512]{2,1,0:T(8,128)(2,1)} %param.12) | copy-start | bytes 1179652
  73.7 7.6 %collective-permute-start.6 = (f32[1,8,64]{2,1,0:T(8,128)S(1)}, f32[1,8,64]{2,1,0:T(8,128)S(1)}, u32[]{:S(2)}, u32[]{:S(2)}) collective-permute-start(f32[1,8,64]{2,1,0:T(8,128)S(1)} %slice.176), channel_id=1, source_target_pairs={{0,8},{8,16},{16,24},{24,32},{32,40},{40,48},{48,56},{56,64},{64,7... | collective-permute-start | bytes 6152 | tf_op jit(solution)/shard_map/ppermute | solution.py:16
  82.8 14.4 %copy-start.4 = (bf16[512,64]{0,1:T(8,128)(2,1)S(1)}, bf16[512,64]{0,1:T(8,128)(2,1)}, u32[]{:S(2)}) copy-start(bf16[512,64]{0,1:T(8,128)(2,1)} %param.19) | copy-start | bytes 196612
  82.8 39.8 %copy-start.6 = (f32[64,64]{1,0:T(8,128)S(1)}, f32[64,64]{1,0:T(8,128)}, u32[]{:S(2)}) copy-start(f32[64,64]{1,0:T(8,128)} %param.23) | copy-start | bytes 49156
  82.8 172.9 %copy-start.5 = (bf16[64,512]{1,0:T(8,128)(2,1)S(1)}, bf16[64,512]{1,0:T(8,128)(2,1)}, u32[]{:S(2)}) copy-start(bf16[64,512]{1,0:T(8,128)(2,1)} %param.20) | copy-start | bytes 196612
  98.5 22.9 %all-to-all-start.1 = ((f32[64,1,128]{2,1,0:T(1,128)}), f32[64,1,128]{2,1,0:T(1,128)S(1)}, u32[]{:S(2)}, u32[]{:S(2)}) async-start(f32[64,1,128]{2,1,0:T(1,128)} %reshape.86), calls=%async_computation.1 | async-start | bytes 65536 | tf_op jit(solution)/shard_map/all_to_all | solution.py:102
  107.9 145.7 %all-gather.3.cloned.1.call-start = ((), (), s32[]{:S(2)}) async-start(), calls=%async_computation.2 | async-start | bytes 2129920 | tf_op jit(solution)/shard_map/all_gather | solution.py:112
  256.3 8.4 %collective-permute-start.9 = (f32[1,8,64]{2,1,0:T(8,128)S(1)}, f32[1,8,64]{2,1,0:T(8,128)S(1)}, u32[]{:S(2)}, u32[]{:S(2)}) collective-permute-start(f32[1,8,64]{2,1,0:T(8,128)S(1)} %slice.187), channel_id=1, source_target_pairs={{8,0},{16,8},{24,16},{32,24},{40,32},{48,40},{56,48},{64,56},{72,6... | collective-permute-start | bytes 6152 | tf_op jit(solution)/shard_map/ppermute | solution.py:19
  262.8 7.6 %collective-permute-start.8 = (f32[1,8,64]{2,1,0:T(8,128)S(1)}, f32[1,8,64]{2,1,0:T(8,128)S(1)}, u32[]{:S(2)}, u32[]{:S(2)}) collective-permute-start(f32[1,8,64]{2,1,0:T(8,128)S(1)} %slice.183), channel_id=1, source_target_pairs={{0,8},{8,16},{16,24},{24,32},{32,40},{40,48},{48,56},{56,64},{64,7... | collective-permute-start | bytes 6152 | tf_op jit(solution)/shard_map/ppermute | solution.py:16
Sparse Core Ops, SparseCore 0:
  123.6 129.8 all-gather.2
